TPU v7x, 1024 devices: a whole 8x8x8 slice. The times are simulated.
1024 devices in a mesh: grp: 16 (over z, core), own: 64 (over x, y).
Axes of the slice: x: 8, y: 8, z: 8, core: 2. Of those that a mesh axis runs over, the one named last changes fastest.
Arguments:
- embeddings: bfloat16 [262144, 1024], P(('grp', 'own')), may hold values from -180 to 180
- coarse_id: int32 [262144], P(('grp', 'own')), may hold values from 0 to 511, as said below
- fine_count: int32 [64, 8], P('own'), may hold values from 1 to 128, 512 in all within a row
- fine: bfloat16 [32768, 1024], P('own'), may hold values from -6 to 6
Outputs:
- fine_new: bfloat16 [32768, 1024], P('own')
- coarse_new: bfloat16 [512, 1024], P('own', 'grp')
Inputs may be any that keep to these rules, and one draw needn't show every extreme that they name: `coarse_id`: among the rows of one device, at most 8 name coarse clusters of one owner (o * 8 to (o + 1) * 8 - 1), and for some owner exactly 8 do. `fine_count`: each row sums to 512; some range holds exactly 128.
All inputs are finite; a program needn't handle non-finite values.
Results may differ from a plain program's by a relative error of at most 0.015.
Values may be sent and summed in bfloat16 or wider, within the bound.
A program may use at most 32 MiB of HBM per device.

v0:
```python
import jax
import jax.numpy as jnp
from jax import lax
from jax.sharding import PartitionSpec as P

KC_OWN = 8


def fine_clusters(lengths, count):
    starts = jnp.cumsum(lengths) - lengths
    index = jnp.arange(count, dtype=jnp.int32)
    inside = (index[:, None] >= starts[None, :]).astype(jnp.int32)
    return jnp.sum(inside, axis=1) - 1


def respond(rows, label, shard, cluster):
    member = cluster[None, :] == label[:, None]
    squares = jnp.sum(jnp.square(shard.astype(jnp.float32)), axis=1)
    dots = lax.dot_general(
        rows, shard, (((1,), (1,)), ((), ())), preferred_element_type=jnp.float32
    )
    scores = (dots - 0.5 * squares[None, :]) * rows.shape[1] ** (-0.5)
    masked = jnp.where(member, scores, -1e30)
    top = jnp.max(masked, axis=1, keepdims=True)
    weights = jnp.where(member, jnp.exp(masked - top), 0.0)
    total = jnp.sum(weights, axis=1, keepdims=True)
    valid = (label >= 0).astype(jnp.float32)
    resp = (weights / (total + (1.0 - valid)[:, None])).astype(jnp.bfloat16)
    sums = lax.dot_general(resp, rows, (((0,), (0,)), ((), ())), preferred_element_type=jnp.float32)
    counts = jnp.sum(resp.astype(jnp.float32), axis=0)
    return (sums, counts)


def update(sums, counts, fine_cols, cluster):
    member = (cluster[None, :] == jnp.arange(KC_OWN, dtype=jnp.int32)[:, None]).astype(jnp.float32)
    numer = sums + fine_cols.astype(jnp.float32)
    weight = counts + 1.0
    fine_next = (numer / weight[:, None]).astype(jnp.bfloat16)
    coarse_num = jnp.dot(member, numer, precision=lax.Precision.HIGHEST)
    coarse_den = jnp.dot(member, weight, precision=lax.Precision.HIGHEST)
    return (fine_next, (coarse_num / coarse_den[:, None]).astype(jnp.bfloat16))


def per_device(embeddings, coarse_id, fine_count, fine):
    owners = lax.axis_size("own")
    rows_dev, width = embeddings.shape
    capacity = max(2, 2 * rows_dev // owners)
    owner = coarse_id // KC_OWN
    onehot = (owner[:, None] == jnp.arange(owners, dtype=jnp.int32)[None, :]).astype(jnp.int32)
    position = jnp.sum((jnp.cumsum(onehot, axis=0) - 1) * onehot, axis=1)
    slot = owner * capacity + position
    outgoing = jnp.zeros((owners * capacity, width), jnp.bfloat16).at[slot].set(embeddings)
    outgoing = outgoing.reshape(owners, capacity, width)
    local_label = (coarse_id - owner * KC_OWN).astype(jnp.float32)
    labels = jnp.full((owners * capacity,), -1.0, jnp.float32).at[slot].set(local_label)
    labels = labels.astype(jnp.bfloat16).reshape(owners, capacity)
    incoming, tags = (
        lax.all_to_all(outgoing, "own", split_axis=0, concat_axis=0, tiled=True),
        lax.all_to_all(labels, "own", split_axis=0, concat_axis=0, tiled=True),
    )
    rows = incoming.reshape(owners * capacity, width)
    label = tags.reshape(owners * capacity).astype(jnp.float32).astype(jnp.int32)
    cluster = fine_clusters(fine_count[0], fine.shape[0])
    sums, counts = respond(rows, label, fine, cluster)
    counts = lax.psum(counts, "grp")
    groups = lax.axis_size("grp")
    share_width = width // groups
    total = lax.psum(sums.astype(jnp.bfloat16), "grp").astype(jnp.float32)
    fine_new, coarse_full = update(total, counts, fine, cluster)
    coarse_new = lax.dynamic_slice_in_dim(
        coarse_full, lax.axis_index("grp") * share_width, share_width, 1
    )
    return (fine_new, coarse_new)


def solution(mesh):
    placed = (P(("grp", "own"), None), P(("grp", "own")), P("own", None), P("own", None))
    return jax.shard_map(
        per_device,
        mesh=mesh,
        in_specs=placed,
        out_specs=(P("own", None), P("own", "grp")),
        check_vma=False,
    )
```

profile of v0, /device:TPU:1, one launch (start us, length us, event | category | flops | bytes accessed | tf_op | source)
XLA Modules:
  0.0 214.2 jit_solution(12491882532500935000)
XLA Ops:
  7.2 0.7 subtract_convert_fusion
  7.9 0.6 reduce-window.9
  8.5 0.2 slice_reduce_fusion
  8.7 0.1 fusion.10
  8.8 1.4 scatter_custom_fusion
  10.2 0.7 all_to_all.12
  10.9 14.0 %all-to-all-start = ((bf16[64,1,8]{2,1,0:T(2,128)(2,1)}), bf16[64,1,8]{2,1,0:T(2,128)(2,1)S(1)}, u32[]{:S(2)}, u32[]{:S(2)}) async-start(bf16[64,1,8]{2,1,0:T(2,128)(2,1)} %all_to_all.12), calls=%async_computation | async-start | bytes 65536 | tf_op jit(solution)/shard_map/all_to_all | solution.py:59
  25.0 3.1 %scatter_custom_fusion.1 = bf16[512,1024]{1,0:T(8,128)(2,1)} fusion(s32[256]{0:T(256)S(1)} %compare_select_fusion.1, bf16[256,1024]{1,0:T(8,128)(2,1)} %param.4, bf16[]{:T(256)} %constant.49.clone.1), kind=kCustom, calls=%fused_computation.18 | custom fusion | bytes 1049088 | tf_op jit(solution)/shard_map/scatter | solution.py:52
  28.1 7.7 %all-to-all-done = bf16[64,1,8]{2,1,0:T(2,128)(2,1)S(1)} async-done(((bf16[64,1,8]{2,1,0:T(2,128)(2,1)}), bf16[64,1,8]{2,1,0:T(2,128)(2,1)S(1)}, u32[]{:S(2)}, u32[]{:S(2)}) %all-to-all-start) | async-done | bytes 1056 | tf_op jit(solution)/shard_map/all_to_all | solution.py:59
  35.8 4.8 %all-to-all-start.1 = ((bf16[64,8,1024]{2,1,0:T(8,128)(2,1)}), bf16[64,8,1024]{2,1,0:T(8,128)(2,1)S(1)}, u32[]{:S(2)}, u32[]{:S(2)}) async-start(bf16[64,8,1024]{2,1,0:T(8,128)(2,1)} %bitcast.3), calls=%async_computation.1 | async-start | bytes 2097152 | tf_op jit(solution)/shard_map/all_to_all | solution.py:58
  40.7 0.2 reduce-window_clone.1
  41.0 0.3 fusion
  41.3 0.1 convert_reduce_fusion.1
  41.5 21.6 %all-to-all-done.1 = bf16[64,8,1024]{2,1,0:T(8,128)(2,1)S(1)} async-done(((bf16[64,8,1024]{2,1,0:T(8,128)(2,1)}), bf16[64,8,1024]{2,1,0:T(8,128)(2,1)S(1)}, u32[]{:S(2)}, u32[]{:S(2)}) %all-to-all-start.1) | async-done | bytes 1048608 | tf_op jit(solution)/shard_map/all_to_all | solution.py:58
  63.0 0.8 fusion.17
  63.8 0.2 fusion.6
  64.1 0.4 convert_reduce_fusion
  64.4 1.7 convolution_convert_fusion
  66.1 43.6 %psum.15 = f32[512]{0:T(512)S(1)} all-reduce(f32[512]{0:T(512)S(1)} %get-tuple-element.2), channel_id=1, replica_groups=mesh['grp'=16,'own'=64] {'grp'}, use_global_device_ids=true, to_apply=%region_12.13 | all-reduce | flops 512 | bytes 4096 | tf_op jit(solution)/shard_map/psum | solution.py:65
  109.8 0.1 convolution_bitcast_fusion
  109.9 93.1 %all-reduce.2.cloned.1.call-done = bf16[512,1024]{1,0:T(8,128)(2,1)} async-done(((bf16[512,1024]{1,0:T(8,128)(2,1)}), bf16[512,1024]{1,0:T(8,128)(2,1)}) %all-reduce.2.cloned.1.call-update) | async-done | bytes 1048592 | tf_op jit(solution)/shard_map/psum | solution.py:68
  203.0 2.3 %fusion.1 = f32[8,1024]{1,0:T(8,128)S(1)} fusion(bf16[512,1024]{1,0:T(8,128)(2,1)S(1)} %copy-done, bf16[512,1024]{1,0:T(8,128)(2,1)} %all-reduce.2.cloned.1.call-done, s32[512]{0:T(512)S(1)} %broadcast_add_fusion.1), kind=kOutput, calls=%fused_computation.6 | convolution fusion | flops 51908608 | bytes 2131968 | tf_op jit(solution)/shard_map/dot_general | solution.py:39
  205.2 0.7 fusion.14
  205.9 1.5 divide_convert_fusion
  (20 shorter events, 0.3 us)
Async XLA Ops:
  10.9 24.9 %all-to-all-start = ((bf16[64,1,8]{2,1,0:T(2,128)(2,1)}), bf16[64,1,8]{2,1,0:T(2,128)(2,1)S(1)}, u32[]{:S(2)}, u32[]{:S(2)}) async-start(bf16[64,1,8]{2,1,0:T(2,128)(2,1)} %all_to_all.12), calls=%async_computation | async-start | bytes 65536 | tf_op jit(solution)/shard_map/all_to_all | solution.py:59
  35.8 4.9 %copy-start.2 = (s32[1,8]{1,0:T(1,128)S(1)}, s32[1,8]{1,0:T(1,128)}, u32[]{:S(2)}) copy-start(s32[1,8]{1,0:T(1,128)} %param.6) | copy-start | bytes 100
  35.8 5.1 %copy-start = (bf16[512,1024]{1,0:T(8,128)(2,1)S(1)}, bf16[512,1024]{1,0:T(8,128)(2,1)}, u32[]{:S(2)}) copy-start(bf16[512,1024]{1,0:T(8,128)(2,1)} %param.7) | copy-start | bytes 3145732
  35.8 27.2 %all-to-all-start.1 = ((bf16[64,8,1024]{2,1,0:T(8,128)(2,1)}), bf16[64,8,1024]{2,1,0:T(8,128)(2,1)S(1)}, u32[]{:S(2)}, u32[]{:S(2)}) async-start(bf16[64,8,1024]{2,1,0:T(8,128)(2,1)} %bitcast.3), calls=%async_computation.1 | async-start | bytes 2097152 | tf_op jit(solution)/shard_map/all_to_all | solution.py:58
  40.6 162.3 %all-reduce.2.cloned.1.call-start = ((), (), s32[]{:S(2)}) async-start(), calls=%async_computation.2 | async-start | bytes 2097152 | tf_op jit(solution)/shard_map/psum | solution.py:68
  203.0 2.9 %copy-start.1 = (bf16[512,1024]{1,0:T(8,128)(2,1)S(1)}, bf16[512,1024]{1,0:T(8,128)(2,1)}, u32[]{:S(2)}) copy-start(bf16[512,1024]{1,0:T(8,128)(2,1)} %all-reduce.2.cloned.1.call-done) | copy-start | bytes 3145732
Sparse Core Ops, SparseCore 0:
  66.3 136.6 all-reduce.1
where the time goes:
time: 215 us; the launch traced here: 214 us
  waiting for transfers between devices  122 us (57%)
  blocking collectives  43.6 us (20%)
  starting transfers between devices  18.9 us (9%)
  between operations  14.1 us (7%)
  local copies, waits for them, and re-layouts  5.54 us (3%)
  other arithmetic  4.87 us (2%)
  matrix products  4.87 us (2%)
    psum x1, waiting for transfers between devices, per_device(): total = lax.psum(sums.astype(jnp.bfloat16), 'grp').astype(jnp.float32)  93.1 us
    psum x1, blocking collectives, per_device(): counts = lax.psum(counts, 'grp')  43.6 us
    all_to_all x1, waiting for transfers between devices, per_device(): lax.all_to_all(outgoing, 'own', split_axis=0, concat_axis=0, tiled=True)  21.6 us
    all_to_all x1, starting transfers between devices, per_device(): lax.all_to_all(labels, 'own', split_axis=0, concat_axis=0, tiled=True)  14 us
    all_to_all x1, waiting for transfers between devices, per_device(): lax.all_to_all(labels, 'own', split_axis=0, concat_axis=0, tiled=True)  7.67 us
    all_to_all x1, starting transfers between devices, per_device(): lax.all_to_all(outgoing, 'own', split_axis=0, concat_axis=0, tiled=True)  4.79 us
  transfers between devices with their start and end apart: 3, of which 3 were waited for; matrix products, arithmetic and copies ran while one was open for 2% of the time, Pallas kernels for 0%

commit v1 on v0

v1 whole, which is shorter than its diff:
```python
import functools

import jax
import jax.numpy as jnp
from jax import lax
from jax.experimental import pallas as pl
from jax.experimental.pallas import tpu as pltpu
from jax.sharding import PartitionSpec as P

KC_OWN = 8
CAP = 8
LANES = 128


def torus(owners):
    fast = 1
    while fast * fast < owners:
        fast *= 2
    return owners // fast, fast


def iota(shape, dim):
    return lax.broadcasted_iota(jnp.int32, shape, dim)


def to_column(row):
    n = row.shape[1]
    return jnp.sum(jnp.where(iota((n, n), 0) == iota((n, n), 1), row, 0.0), axis=1, keepdims=True)


def kernel(
    owners, groups,
    emb, cid, fine_count, fine,
    fine_new, coarse_new,
    out_rows, in_rows, out_tags, in_tags, rows, resp, own_part, sib_out, sib_in,
    right_out, right_in, left_out, left_in, cnt_out, cnt_in, num_out, num_in, table,
    send_rows, recv_rows, send_tags, recv_tags, send_sib, recv_sib,
    send_right, recv_right, send_left, recv_left, send_cnt, recv_cnt, send_num, recv_num,
    send_gr, recv_gr, send_gl, recv_gl, send_gs, recv_gs, send_home,
):
    nx, ny = torus(owners)
    nz = groups // 2
    rows_dev, width = emb.shape
    half = width // 2
    f_own = fine.shape[0]
    f_half = f_own // 2
    chunk = min(16, owners)
    chunks = owners // chunk
    slots = chunk * CAP
    right_steps, left_steps = nz // 2, nz // 2 - 1
    bf16, f32 = jnp.bfloat16, jnp.float32

    own = lax.axis_index("own")
    grp = lax.axis_index("grp")
    mx, my = own // ny, own % ny
    z, core = grp // 2, grp % 2
    sibling = {"grp": z * 2 + 1 - core}
    right = {"grp": lax.rem(z + 1, nz) * 2 + core}
    left = {"grp": lax.rem(z + nz - 1, nz) * 2 + core}

    def peer(i):
        kx, b = lax.rem(i, nx), i // nx
        ky = lax.rem(3 * kx + b, ny)
        return {"own": lax.rem(mx + kx, nx) * ny + lax.rem(my + ky, ny)}

    def mate(i):
        return {"grp": lax.rem(grp + i, groups)}

    def remote(src, dst, send, recv, device):
        return pltpu.make_async_remote_copy(
            src_ref=src, dst_ref=dst, send_sem=send, recv_sem=recv,
            device_id=device, device_id_type=pl.DeviceIdType.MESH,
        )

    def take(ref, sem):
        pltpu.make_async_copy(ref, ref, sem).wait()

    barrier = pltpu.get_barrier_semaphore()

    @pl.loop(1, owners)
    def _(i):
        pl.semaphore_signal(barrier, inc=1, device_id=peer(i), device_id_type=pl.DeviceIdType.MESH)

    @pl.loop(1, groups)
    def _(i):
        pl.semaphore_signal(barrier, inc=1, device_id=mate(i), device_id_type=pl.DeviceIdType.MESH)

    ids = cid[...]
    owner = lax.shift_right_logical(ids, 3)
    kx = (lax.shift_right_logical(owner, ny.bit_length() - 1) - mx) & (nx - 1)
    ky = ((owner & (ny - 1)) - my) & (ny - 1)
    block = ((ky - 3 * kx) & (ny - 1)) * nx + kx
    owner_row = owner.astype(f32)
    owner_col = to_column(owner_row)
    local_col = to_column((ids & (KC_OWN - 1)).astype(f32))
    square = (rows_dev, rows_dev)
    same = owner_col == owner_row
    place_row = jnp.sum(jnp.where(same & (iota(square, 0) < iota(square, 1)), 1.0, 0.0), axis=0, keepdims=True)
    place_col = jnp.sum(jnp.where(same & (iota(square, 1) < iota(square, 0)), 1.0, 0.0), axis=1, keepdims=True)
    target = block * (2 * CAP) + place_row.astype(jnp.int32)

    pick = (iota((owners, rows_dev), 0) == block).astype(bf16)
    lane = (iota((rows_dev, LANES), 1) & (CAP - 1)).astype(f32)
    spread = jnp.where(place_col == lane, local_col + 1.0, 0.0).astype(bf16)
    tags = jnp.dot(pick, spread, preferred_element_type=f32)
    out_tags[...] = tags.reshape(owners, 1, LANES)
    in_tags[0] = out_tags[0]

    def build(c):
        tall = 2 * CAP * chunk
        at = iota((tall, rows_dev), 0) + c * tall
        low = (at == target).astype(bf16)
        high = (at == target + CAP).astype(bf16)
        made = jnp.dot(low, emb[:, :half], preferred_element_type=f32)
        made += jnp.dot(high, emb[:, half:], preferred_element_type=f32)
        out_rows[pl.ds(c * chunk, chunk)] = made.astype(bf16).reshape(chunk, 2 * CAP, half)

    build(0)
    pl.semaphore_wait(barrier, owners + groups - 2)
    for c in range(chunks):
        if c > 0:
            build(c)

        @pl.loop(max(1, c * chunk), (c + 1) * chunk)
        def _(i):
            remote(out_tags.at[i], in_tags.at[i], send_tags.at[0], recv_tags.at[c], peer(i)).start()
            remote(out_rows.at[i], in_rows.at[i], send_rows.at[0], recv_rows.at[c], peer(i)).start()

    in_rows[0] = out_rows[0]

    fine_rows = fine[...].astype(f32)
    squares = jnp.sum(fine_rows * fine_rows, axis=1, keepdims=True)
    index_col, index_row = iota((f_own, 1), 0), iota((1, f_own), 1)
    cluster_col = jnp.zeros((f_own, 1), jnp.int32)
    cluster_row = jnp.zeros((1, f_own), jnp.int32)
    start = jnp.int32(0)
    for k in range(KC_OWN - 1):
        start = start + fine_count[0, k]
        cluster_col += (index_col >= start).astype(jnp.int32)
        cluster_row += (index_row >= start).astype(jnp.int32)
    table[...] = jnp.broadcast_to(squares * 0.5, table.shape)
    cluster_of = cluster_col.astype(f32)
    member_of = (cluster_row == iota((KC_OWN, f_own), 0)).astype(f32)

    for c in range(chunks):
        lo = max(1, c * chunk)
        part = pl.ds(lo, (c + 1) * chunk - lo)
        take(in_tags.at[part], recv_tags.at[c])
        take(in_rows.at[part], recv_rows.at[c])
        here = pl.ds(c * chunk, chunk)
        tag = in_tags[here].reshape(chunk, LANES)[:, :slots]
        tag = jnp.where(iota((chunk, slots), 1) // CAP == iota((chunk, slots), 0), tag, 0.0)
        label = jnp.sum(tag, axis=0, keepdims=True) - 1.0
        wide = in_rows[here].astype(f32).reshape(chunk, 2, CAP, half)
        low = wide[:, 0].reshape(slots, half).astype(bf16)
        high = wide[:, 1].reshape(slots, half).astype(bf16)
        at = pl.ds(c * slots, slots)
        for b in range(nz // 2):
            rows[b, at, :] = low[:, b * LANES:(b + 1) * LANES]
            rows[nz // 2 + b, at, :] = high[:, b * LANES:(b + 1) * LANES]
        flip = (((1,), (1,)), ((), ()))
        dots = lax.dot_general(fine[:, :half], low, flip, preferred_element_type=f32)
        dots += lax.dot_general(fine[:, half:], high, flip, preferred_element_type=f32)
        member = cluster_of == label
        scores = (dots - table[:, :slots]) * (width ** -0.5)
        masked = jnp.where(member, scores, -1e30)
        top = jnp.max(masked, axis=0, keepdims=True)
        weights = jnp.where(member, jnp.exp(masked - top), 0.0)
        total = jnp.sum(weights, axis=0, keepdims=True)
        empty = (label < 0.0).astype(f32)
        resp[:, at] = (weights / (total + empty)).astype(bf16)

    mine, other = pl.ds(core * f_half, f_half), pl.ds((1 - core) * f_half, f_half)
    order = []
    for t in range(right_steps):
        order.append(right_steps - t)
        if t < left_steps:
            order.append(nz - left_steps + t)
    order.append(0)
    for off in order:
        b = lax.rem(z + off, nz)
        sib_out[b] = jnp.dot(resp[other, :], rows[b], preferred_element_type=f32).astype(bf16)
        remote(sib_out.at[b], sib_in.at[b], send_sib.at[b], recv_sib.at[b], sibling).start()
        own_part[b] = jnp.dot(resp[mine, :], rows[b], preferred_element_type=f32)

    ones = jnp.ones((8, resp.shape[1]), bf16)
    counts = lax.dot_general(ones, resp[...], (((1,), (1,)), ((), ())), preferred_element_type=f32)
    cnt_out[...] = counts[0:1, :]
    cnt_in[0] = counts[0:1, :]

    @pl.loop(1, groups)
    def _(i):
        remote(cnt_out, cnt_in.at[i], send_cnt.at[0], recv_cnt.at[0], mate(i)).start()

    def chip(b):
        take(sib_in.at[b], recv_sib.at[b])
        return own_part[b] + sib_in[b].astype(f32)

    for t in range(right_steps):
        total = chip(lax.rem(z + right_steps - t, nz))
        if t > 0:
            take(right_in.at[t - 1], recv_right.at[t - 1])
            total += right_in[t - 1].astype(f32)
        right_out[t] = total.astype(bf16)
        remote(right_out.at[t], right_in.at[t], send_right.at[t], recv_right.at[t], right).start()
        if t < left_steps:
            total = chip(lax.rem(z + nz - left_steps + t, nz))
            if t > 0:
                take(left_in.at[t - 1], recv_left.at[t - 1])
                total += left_in[t - 1].astype(f32)
            left_out[t] = total.astype(bf16)
            remote(left_out.at[t], left_in.at[t], send_left.at[t], recv_left.at[t], left).start()

    take(cnt_in.at[pl.ds(1, groups - 1)], recv_cnt.at[0])
    count = jnp.sum(cnt_in[...], axis=0)
    weight = count + 1.0
    count_half = jnp.where(core == 0, weight[:, :f_half], weight[:, f_half:])
    weight_col = to_column(count_half)
    den = jnp.sum(member_of * weight, axis=1, keepdims=True)
    member_half = jnp.where(core == 0, member_of[:, :f_half], member_of[:, f_half:])

    columns = pl.ds(pl.multiple_of(z * LANES, LANES), LANES)
    numer = chip(z) + fine[mine, columns].astype(f32)
    if left_steps > 0:
        take(left_in.at[left_steps - 1], recv_left.at[left_steps - 1])
        numer += left_in[left_steps - 1].astype(f32)
    take(right_in.at[right_steps - 1], recv_right.at[right_steps - 1])
    numer += right_in[right_steps - 1].astype(f32)
    fine_new[mine, columns] = (numer / weight_col).astype(bf16)

    def spot(b):
        return fine_new.at[mine, pl.ds(pl.multiple_of(b * LANES, LANES), LANES)]

    def to_sibling(b):
        remote(spot(b), spot(b), send_gs.at[0], recv_gs.at[0], sibling).start()

    def to_right(t):
        b = lax.rem(z + nz - t, nz)
        remote(spot(b), spot(b), send_gr.at[t], recv_gr.at[t], right).start()

    def to_left(t):
        b = lax.rem(z + t, nz)
        remote(spot(b), spot(b), send_gl.at[t], recv_gl.at[t], left).start()

    to_right(0)
    if left_steps > 0:
        to_left(0)
    to_sibling(z)

    num = lax.dot_general(
        member_half, numer, (((1,), (0,)), ((), ())),
        preferred_element_type=f32, precision=lax.Precision.HIGHEST,
    )
    num_out[...] = num
    remote(num_out, num_in, send_num.at[0], recv_num.at[0], sibling).start()

    for t in range(right_steps):
        b = lax.rem(z + nz - 1 - t, nz)
        take(spot(b), recv_gr.at[t])
        if t + 1 < right_steps:
            to_right(t + 1)
        to_sibling(b)
        if t < left_steps:
            b = lax.rem(z + 1 + t, nz)
            take(spot(b), recv_gl.at[t])
            if t + 1 < left_steps:
                to_left(t + 1)
            to_sibling(b)

    take(num_in, recv_num.at[0])
    coarse = (num + num_in[...]) / den
    coarse = jnp.where(core == 0, coarse[:, :LANES // 2], coarse[:, LANES // 2:])
    coarse_new[...] = coarse.astype(bf16)

    take(out_rows.at[pl.ds(1, owners - 1)], send_rows.at[0])
    take(out_tags.at[pl.ds(1, owners - 1)], send_tags.at[0])
    take(cnt_in.at[pl.ds(1, groups - 1)], send_cnt.at[0])
    take(num_out, send_num.at[0])
    for b in range(nz):
        take(sib_out.at[b], send_sib.at[b])
    for t in range(right_steps):
        take(right_out.at[t], send_right.at[t])
        take(spot(0), send_gr.at[t])
    for t in range(left_steps):
        take(left_out.at[t], send_left.at[t])
        take(spot(0), send_gl.at[t])
    take(fine_new.at[mine, :], send_gs.at[0])
    take(fine_new.at[other, :], recv_gs.at[0])


def per_device(owners, groups, embeddings, coarse_id, fine_count, fine):
    rows_dev, width = embeddings.shape
    f_own = fine.shape[0]
    nz = groups // 2
    assert width == nz * LANES
    right_steps, left_steps = nz // 2, nz // 2 - 1
    chunk = min(16, owners)
    chunks = owners // chunk
    slots = owners * CAP
    bf16, f32 = jnp.bfloat16, jnp.float32
    vmem, dma = pltpu.VMEM, pltpu.SemaphoreType.DMA
    in_vmem = pl.BlockSpec(memory_space=pltpu.VMEM)
    piece = (f_own // 2, LANES)
    return pl.pallas_call(
        functools.partial(kernel, owners, groups),
        out_shape=(
            jax.ShapeDtypeStruct((f_own, width), bf16),
            jax.ShapeDtypeStruct((KC_OWN, width // groups), bf16),
        ),
        in_specs=[in_vmem, in_vmem, pl.BlockSpec(memory_space=pltpu.SMEM), in_vmem],
        out_specs=(in_vmem, in_vmem),
        scratch_shapes=[
            vmem((owners, 2 * CAP, width // 2), bf16),
            vmem((owners, 2 * CAP, width // 2), bf16),
            vmem((owners, 1, LANES), f32),
            vmem((owners, 1, LANES), f32),
            vmem((nz, slots, LANES), bf16),
            vmem((f_own, slots), bf16),
            vmem((nz,) + piece, f32),
            vmem((nz,) + piece, bf16),
            vmem((nz,) + piece, bf16),
            vmem((right_steps,) + piece, bf16),
            vmem((right_steps,) + piece, bf16),
            vmem((max(1, left_steps),) + piece, bf16),
            vmem((max(1, left_steps),) + piece, bf16),
            vmem((1, f_own), f32),
            vmem((groups, 1, f_own), f32),
            vmem((KC_OWN, LANES), f32),
            vmem((KC_OWN, LANES), f32),
            vmem((f_own, LANES), f32),
            dma((1,)), dma((chunks,)), dma((1,)), dma((chunks,)), dma((nz,)), dma((nz,)),
            dma((right_steps,)), dma((right_steps,)), dma((max(1, left_steps),)), dma((max(1, left_steps),)),
            dma((1,)), dma((1,)), dma((1,)), dma((1,)),
            dma((right_steps,)), dma((right_steps,)), dma((max(1, left_steps),)), dma((max(1, left_steps),)),
            dma((1,)), dma((1,)), dma((1,)),
        ],
        compiler_params=pltpu.CompilerParams(
            collective_id=0, has_side_effects=True, vmem_limit_bytes=40 * 1024 * 1024
        ),
    )(embeddings, coarse_id.reshape(1, rows_dev), fine_count, fine)


def solution(mesh):
    return jax.shard_map(
        functools.partial(per_device, mesh.shape["own"], mesh.shape["grp"]),
        mesh=mesh,
        in_specs=(P(("grp", "own"), None), P(("grp", "own")), P("own", None), P("own", None)),
        out_specs=(P("own", None), P("own", "grp")),
        check_vma=False,
    )
```

time: 215 us -> 93 us (0.43)
  waiting for transfers between devices: 122 us -> 0 us
  Pallas kernels: 0 us -> 87.6 us
  blocking collectives: 43.6 us -> 0 us
  starting transfers between devices: 18.9 us -> 0 us
  between operations: 14.1 us -> 0.66 us
  matrix products: 4.87 us -> 0 us
  other arithmetic: 4.87 us -> 0 us
    psum x1 -> x0, waiting for transfers between devices: 93.1 us -> none  [per_device(): total = lax.psum(sums.astype(jnp.bfloat16), 'grp').astype(jnp.float32)]
    pallas_call x0 -> x1, Pallas kernels: none -> 87.6 us  [per_device(): pl.pallas_call(functools.partial(kernel, owners, groups), out_shape=(jax....]
    psum x1 -> x0, blocking collectives: 43.6 us -> none  [per_device(): counts = lax.psum(counts, 'grp')]
    all_to_all x2 -> x0, waiting for transfers between devices: 29.2 us -> none  [the longest x1 21.6 us: per_device(): lax.all_to_all(outgoing, 'own', split_axis=0, concat_axis=0, tiled=True)]
    all_to_all x2 -> x0, starting transfers between devices: 18.8 us -> none  [the longest x1 14 us: per_device(): lax.all_to_all(labels, 'own', split_axis=0, concat_axis=0, tiled=True)]
    dot_general x4 -> x0, matrix products: 4.87 us -> none  [the longest x1 2.28 us: update(): coarse_num = jnp.dot(member, numer, precision=lax.Precision.HIGHEST)]
    scatter x2 -> x0, local copies, waits for them, and re-layouts: 4.54 us -> none  [the longest x1 3.15 us: per_device(): jnp.zeros((owners * capacity, width), jnp.bfloat16).at[slot].set(embeddings)]
    unnamed x6 -> x10, local copies, waits for them, and re-layouts: 0.01 us -> 4.49 us
  transfers between devices with their start and end apart: 3 -> 0, of which waited for: 3 -> 0; matrix products, arithmetic and copies ran while one was open for 2% -> 0% of each run, Pallas kernels for 0% -> 0%
where the time goes in v1:
time: 93 us; the launch traced here: 92.7 us
  Pallas kernels  87.6 us (94%)
  local copies, waits for them, and re-layouts  4.49 us (5%)
    pallas_call x1, Pallas kernels, per_device(): pl.pallas_call(functools.partial(kernel, owners, groups), out_shape=(jax....  87.6 us
    unnamed x10, local copies, waits for them, and re-layouts  4.49 us

profile of v1, /device:TPU:1, one launch (start us, length us, event | category | flops | bytes accessed | tf_op | source)
XLA Modules:
  0.0 92.7 jit_solution(14901224375411501272)
XLA Ops:
  0.6 0.0 copy-start.3
  0.6 0.0 copy-start.2
  0.7 0.6 copy-done.3
  1.3 0.0 copy-done.2
  1.3 0.0 copy-start
  1.3 1.2 %copy-done = bf16[512,1024]{1,0:T(8,128)(2,1)S(1)} copy-done((bf16[512,1024]{1,0:T(8,128)(2,1)S(1)}, bf16[512,1024]{1,0:T(8,128)(2,1)}, u32[]{:S(2)}) %copy-start) | copy-done | bytes 1048600
  2.6 0.0 copy-start.1
  2.6 1.0 %copy-done.1 = bf16[256,1024]{1,0:T(8,128)(2,1)S(1)} copy-done((bf16[256,1024]{1,0:T(8,128)(2,1)S(1)}, bf16[256,1024]{1,0:T(8,128)(2,1)}, u32[]{:S(2)}) %copy-start.1) | copy-done | bytes 524312
  3.6 87.6 %shard_map.59 = (bf16[512,1024]{1,0:T(8,128)(2,1)S(1)}, bf16[8,64]{1,0:T(8,128)(2,1)S(1)}) custom-call(bf16[256,1024]{1,0:T(8,128)(2,1)S(1)} %copy-done.1, s32[1,256]{1,0:T(1,128)S(1)} %bitcast.1, s32[1,8]{1,0:T(1,128)S(1)} %copy-done.3, bf16[512,1024]{1,0:T(8,128)(2,1)S(1)} %copy-done), custom_call_target="tpu_custom_call" | custom-call | tf_op jit(solution)/shard_map/pallas_call | solution.py:304
  91.2 1.0 %copy.8 = bf16[512,1024]{1,0:T(8,128)(2,1)} copy(bf16[512,1024]{1,0:T(8,128)(2,1)S(1)} %get-tuple-element.4) | data formatting | bytes 2097152
  92.1 0.6 copy.9
Async XLA Ops:
  0.6 0.7 copy-start.3
  0.6 0.7 copy-start.2
  1.3 1.2 %copy-start = (bf16[512,1024]{1,0:T(8,128)(2,1)S(1)}, bf16[512,1024]{1,0:T(8,128)(2,1)}, u32[]{:S(2)}) copy-start(bf16[512,1024]{1,0:T(8,128)(2,1)} %fine.1) | copy-start | bytes 3145732
  2.6 1.0 %copy-start.1 = (bf16[256,1024]{1,0:T(8,128)(2,1)S(1)}, bf16[256,1024]{1,0:T(8,128)(2,1)}, u32[]{:S(2)}) copy-start(bf16[256,1024]{1,0:T(8,128)(2,1)} %emb.1) | copy-start | bytes 1572868

commit v2 on v1

v2 whole, which is shorter than its diff:
```python
import functools

import jax
import jax.numpy as jnp
from jax import lax
from jax.experimental import pallas as pl
from jax.experimental.pallas import tpu as pltpu
from jax.sharding import PartitionSpec as P

KC_OWN = 8
CAP = 8
LANES = 128


def torus(owners):
    fast = 1
    while fast * fast < owners:
        fast *= 2
    return owners // fast, fast


def turned(a, b, r):
    return ((a, b), (-b, a), (-a, -b), (b, -a))[r]


def far_first(nx, ny):
    if (nx, ny) != (8, 8):
        return [(i % nx, i // nx) for i in range(nx * ny)]
    order = []
    for g in range(16):
        a, b = 4 - g // 4, 3 - g % 4
        if (a, b) == (4, 0):
            order += [(4, 0), (0, 4), (0, 0), (4, 4)]
        else:
            order += [turned(a, b, r) for r in range(4)]
    return [(a % nx, b % ny) for a, b in order]


def iota(shape, dim):
    return lax.broadcasted_iota(jnp.int32, shape, dim)


def to_column(row):
    n = row.shape[1]
    return jnp.sum(jnp.where(iota((n, n), 0) == iota((n, n), 1), row, 0.0), axis=1, keepdims=True)


def kernel(
    owners, groups,
    emb_hbm, cid_hbm, count_hbm, fine_hbm,
    fine_new, coarse_new,
    emb, cid, fine_count, fine,
    out_rows, in_rows, out_tags, in_tags, rows, resp, own_part, sib_out, sib_in,
    out4, in4, out3, in3, out2, in2, out1, in1, cnt_out, cnt_in, num_out, num_in, table, ring_new,
    load, send_rows, recv_rows, send_tags, recv_tags, send_sib, recv_sib,
    send_sum, recv_sum, send_cnt, recv_cnt, send_num, recv_num, send_ring, recv_ring, send_gs, recv_gs, keep,
):
    nx, ny = torus(owners)
    nz = groups // 2
    rows_dev, width = emb.shape
    half = width // 2
    f_own = fine.shape[0]
    f_half = f_own // 2
    f_quarter = f_own // 4
    chunk = min(16, owners)
    chunks = owners // chunk
    slots = chunk * CAP
    bf16, f32 = jnp.bfloat16, jnp.float32

    own = lax.axis_index("own")
    grp = lax.axis_index("grp")
    mx, my = own // ny, own % ny
    z, core = grp // 2, grp % 2
    sibling = {"grp": z * 2 + 1 - core}

    order = far_first(nx, ny)
    here = order.index((0, 0))

    def peer(kx, ky):
        return {"own": lax.rem(mx + kx + nx, nx) * ny + lax.rem(my + ky + ny, ny)}

    def for_peers(lo, hi, act):
        if (nx, ny) != (8, 8):
            for i in range(lo, hi):
                if i != here:
                    act(i, peer(*order[i]))
            return

        def four(g):
            a, b = 4 - g // 4, 3 - lax.rem(g, 4)
            for r in range(4):
                act(g * 4 + r, peer(*turned(a, b, r)))

        first, last = lo // 4, hi // 4
        if first <= 3 < last:
            pl.loop(first, 3)(four)
            for i in (12, 13, 15):
                act(i, peer(*order[i]))
            first = 4
        pl.loop(first, last)(four)

    def along(k):
        return lax.rem(z + k + nz, nz)

    def at_z(k):
        return {"grp": along(k) * 2 + core}

    def mate(i):
        return {"grp": lax.rem(grp + i, groups)}

    def remote(src, dst, send, recv, device):
        return pltpu.make_async_remote_copy(
            src_ref=src, dst_ref=dst, send_sem=send, recv_sem=recv,
            device_id=device, device_id_type=pl.DeviceIdType.MESH,
        )

    def take(ref, sem):
        pltpu.make_async_copy(ref, ref, sem).wait()

    loads = [
        pltpu.make_async_copy(src, dst, load.at[n])
        for n, (src, dst) in enumerate(
            ((cid_hbm, cid), (emb_hbm, emb), (count_hbm, fine_count), (fine_hbm, fine))
        )
    ]
    for copy in loads:
        copy.start()

    barrier = pltpu.get_barrier_semaphore()

    def greet(i, device):
        pl.semaphore_signal(barrier, inc=1, device_id=device, device_id_type=pl.DeviceIdType.MESH)

    for_peers(0, owners, greet)

    @pl.loop(1, groups)
    def _(i):
        greet(i, mate(i))

    loads[0].wait()
    ids = cid[...]
    owner = lax.shift_right_logical(ids, 3)
    kx = (lax.shift_right_logical(owner, ny.bit_length() - 1) - mx) & (nx - 1)
    ky = ((owner & (ny - 1)) - my) & (ny - 1)
    away = kx * ny + ky
    block = jnp.zeros_like(away)
    for i, (a, b) in enumerate(order):
        block = jnp.where(away == a * ny + b, i, block)
    owner_row = owner.astype(f32)
    owner_col = to_column(owner_row)
    local_col = to_column((ids & (KC_OWN - 1)).astype(f32))
    square = (rows_dev, rows_dev)
    same = owner_col == owner_row
    place_row = jnp.sum(jnp.where(same & (iota(square, 0) < iota(square, 1)), 1.0, 0.0), axis=0, keepdims=True)
    place_col = jnp.sum(jnp.where(same & (iota(square, 1) < iota(square, 0)), 1.0, 0.0), axis=1, keepdims=True)
    target = block * (2 * CAP) + place_row.astype(jnp.int32)

    pick = (iota((owners, rows_dev), 0) == block).astype(bf16)
    lane = (iota((rows_dev, LANES), 1) & (CAP - 1)).astype(f32)
    spread = jnp.where(place_col == lane, local_col + 1.0, 0.0).astype(bf16)
    tags = jnp.dot(pick, spread, preferred_element_type=f32)
    out_tags[...] = tags.reshape(owners, 1, LANES)
    in_tags[here] = out_tags[here]

    loads[1].wait()
    for c in range(chunks):
        tall = 2 * CAP * chunk
        at = iota((tall, rows_dev), 0) + c * tall
        low = (at == target).astype(bf16)
        high = (at == target + CAP).astype(bf16)
        made = jnp.dot(low, emb[:, :half], preferred_element_type=f32)
        made += jnp.dot(high, emb[:, half:], preferred_element_type=f32)
        out_rows[pl.ds(c * chunk, chunk)] = made.astype(bf16).reshape(chunk, 2 * CAP, half)

    pl.semaphore_wait(barrier, owners + groups - 2)
    for c in range(chunks):

        def send(i, device):
            remote(out_tags.at[i], in_tags.at[i], send_tags.at[0], recv_tags.at[c], device).start()
            remote(out_rows.at[i], in_rows.at[i], send_rows.at[0], recv_rows.at[c], device).start()

        for_peers(c * chunk, (c + 1) * chunk, send)

    in_rows[here] = out_rows[here]

    loads[2].wait()
    loads[3].wait()
    fine_rows = fine[...].astype(f32)
    squares = jnp.sum(fine_rows * fine_rows, axis=1, keepdims=True)
    index_col, index_row = iota((f_own, 1), 0), iota((1, f_own), 1)
    cluster_col = jnp.zeros((f_own, 1), f32)
    cluster_row = jnp.zeros((1, f_own), f32)
    start = jnp.zeros((1, 1), jnp.int32)
    for k in range(KC_OWN - 1):
        start = start + fine_count[:, k:k + 1]
        cluster_col += (index_col >= start).astype(f32)
        cluster_row += (index_row >= start).astype(f32)
    table[...] = jnp.broadcast_to(squares * 0.5, table.shape)
    member_of = (cluster_row == iota((KC_OWN, f_own), 0).astype(f32)).astype(f32)

    for c in range(chunks):
        gone = chunk - (1 if c == here // chunk else 0)
        if gone > 0:
            take(in_tags.at[pl.ds(c * chunk, gone)], recv_tags.at[c])
            take(in_rows.at[pl.ds(c * chunk, gone)], recv_rows.at[c])
        these = pl.ds(c * chunk, chunk)
        tag = in_tags[these].reshape(chunk, LANES)[:, :slots]
        tag = jnp.where(iota((chunk, slots), 1) // CAP == iota((chunk, slots), 0), tag, 0.0)
        label = jnp.sum(tag, axis=0, keepdims=True) - 1.0
        wide = in_rows[these].astype(f32).reshape(chunk, 2, CAP, half)
        low = wide[:, 0].reshape(slots, half).astype(bf16)
        high = wide[:, 1].reshape(slots, half).astype(bf16)
        at = pl.ds(c * slots, slots)
        for b in range(nz // 2):
            rows[b, at, :] = low[:, b * LANES:(b + 1) * LANES]
            rows[nz // 2 + b, at, :] = high[:, b * LANES:(b + 1) * LANES]
        flip = (((1,), (1,)), ((), ()))
        dots = lax.dot_general(fine[:, :half], low, flip, preferred_element_type=f32)
        dots += lax.dot_general(fine[:, half:], high, flip, preferred_element_type=f32)
        member = cluster_col == label
        scores = (dots - table[:, :slots]) * (width ** -0.5)
        masked = jnp.where(member, scores, -1e30)
        top = jnp.max(masked, axis=0, keepdims=True)
        weights = jnp.where(member, jnp.exp(masked - top), 0.0)
        total = jnp.sum(weights, axis=0, keepdims=True)
        empty = (label < 0.0).astype(f32)
        resp[:, at] = (weights / (total + empty)).astype(bf16)

    mine, other = pl.ds(core * f_half, f_half), pl.ds((1 - core) * f_half, f_half)

    def weigh(off):
        b = along(off)
        sib_out[b] = jnp.dot(resp[other, :], rows[b], preferred_element_type=f32).astype(bf16)
        remote(sib_out.at[b], sib_in.at[b], send_sib.at[b], recv_sib.at[b], sibling).start()
        own_part[b] = jnp.dot(resp[mine, :], rows[b], preferred_element_type=f32)

    def count_up():
        ones = jnp.ones((8, resp.shape[1]), bf16)
        counts = lax.dot_general(ones, resp[...], (((1,), (1,)), ((), ())), preferred_element_type=f32)
        cnt_out[...] = counts[0:1, :]
        cnt_in[0] = counts[0:1, :]

        @pl.loop(1, groups)
        def _(i):
            remote(cnt_out, cnt_in.at[i], send_cnt.at[0], recv_cnt.at[0], mate(i)).start()

    def chip(off, q):
        piece = pl.ds(q * f_quarter, f_quarter)
        b = along(off)
        return own_part[b, piece, :] + sib_in[b, piece, :].astype(f32)

    def both(off):
        b = along(off)
        take(sib_in.at[b], recv_sib.at[b])
        return own_part[b] + sib_in[b].astype(f32)

    sent = []

    def give(n, src, dst, k):
        remote(src, dst, send_sum.at[n], recv_sum.at[n], at_z(k)).start()
        sent.append((src, send_sum.at[n]))

    def got(n, ref):
        take(ref, recv_sum.at[n])
        return ref[...].astype(f32)

    for off in (4, 3, -3):
        weigh(off)
    total = both(4).astype(bf16)
    for q, k in ((0, -2), (1, 2)):
        out4[q] = total[q * f_quarter:(q + 1) * f_quarter]
        give(q, out4.at[q], in4.at[q], k)
    for n, off, k in ((0, -3, -1), (1, 3, 1)):
        out3[n] = both(off).astype(bf16)
        give(2 + n, out3.at[n], in3.at[n], k)
    for off in (2, -2):
        weigh(off)
    count_up()
    for off in (1, -1):
        weigh(off)
    for n, off in ((0, -1), (1, 1)):
        out1[n] = both(off).astype(bf16)
        give(4 + n, out1.at[n], in1.at[n], off)
    weigh(0)
    for off in (-2, 2, 0):
        take(sib_in.at[along(off)], recv_sib.at[along(off)])
    for n, off in ((0, -2), (1, 2)):
        take(in3.at[n], recv_sum.at[2 + n])
    for q in range(2):
        for n, off in ((1, 2), (0, -2)) if q == 0 else ((0, -2), (1, 2)):
            total = chip(off, q) + in3[n, pl.ds(q * f_quarter, f_quarter), :].astype(f32)
            if n == q:
                total += got(q, in4.at[q])
            out2[n, q] = total.astype(bf16)
            give(6 + 2 * n + q, out2.at[n, q], in2.at[n, q], off)

    take(cnt_in.at[pl.ds(1, groups - 1)], recv_cnt.at[0])
    weight = jnp.sum(cnt_in[...], axis=0) + 1.0
    weight_col = to_column(jnp.where(core == 0, weight[:, :f_half], weight[:, f_half:]))

    ring = []

    def part_of(off, q):
        return ring_new.at[along(off), pl.ds(q * f_quarter, f_quarter), :]

    def spread_to(n, off, q, k):
        piece = part_of(off, q)
        remote(piece, piece, send_ring.at[n], recv_ring.at[n], at_z(k)).start()
        ring.append((piece, send_ring.at[n]))

    def arrived(n, off, q):
        take(part_of(off, q), recv_ring.at[n])

    def hand_over(off):
        b = along(off)
        place = fine_new.at[mine, pl.ds(pl.multiple_of(b * LANES, LANES), LANES)]
        remote(ring_new.at[b], place, send_gs.at[0], recv_gs.at[0], sibling).start()
        pltpu.make_async_copy(ring_new.at[b], place, keep.at[0]).start()

    columns = pl.ds(pl.multiple_of(z * LANES, LANES), LANES)
    numers = []
    for n in range(2):
        take(in1.at[n], recv_sum.at[4 + n])
    for q in range(2):
        piece = pl.ds(q * f_quarter, f_quarter)
        old = fine[pl.ds(pl.multiple_of(core * f_half + q * f_quarter, f_quarter), f_quarter), columns]
        numer = chip(0, q) + old.astype(f32)
        numer += in1[0, piece, :].astype(f32) + in1[1, piece, :].astype(f32)
        numer += got(6 + q, in2.at[0, q]) + got(8 + q, in2.at[1, q])
        numers.append(numer)
        ring_new[z, piece, :] = (numer / weight_col[q * f_quarter:(q + 1) * f_quarter]).astype(bf16)
        spread_to(q, 0, q, 2)
        spread_to(2 + q, 0, q, -2)
    for q in range(2):
        spread_to(4 + q, 0, q, 1)
        spread_to(6 + q, 0, q, -1)
    hand_over(0)

    member_half = jnp.where(core == 0, member_of[:, :f_half], member_of[:, f_half:])
    num = sum(
        lax.dot_general(
            member_half[:, q * f_quarter:(q + 1) * f_quarter], numers[q], (((1,), (0,)), ((), ())),
            preferred_element_type=f32, precision=lax.Precision.HIGHEST,
        )
        for q in range(2)
    )
    num_out[...] = num
    remote(num_out, num_in, send_num.at[0], recv_num.at[0], sibling).start()
    den = jnp.sum(member_of * weight, axis=1, keepdims=True)

    arrived(0, -2, 0)
    spread_to(12, -2, 0, 2)
    spread_to(8, -2, 0, 1)
    arrived(2, 2, 0)
    spread_to(10, 2, 0, -1)
    arrived(3, 2, 1)
    spread_to(13, 2, 1, -2)
    spread_to(11, 2, 1, -1)
    arrived(1, -2, 1)
    spread_to(9, -2, 1, 1)
    hand_over(-2)
    hand_over(2)
    for n, off in ((4, -1), (6, 1)):
        arrived(n, off, 0)
        arrived(n + 1, off, 1)
        hand_over(off)

    take(num_in, recv_num.at[0])
    coarse = (num + num_in[...]) / den
    coarse = jnp.where(core == 0, coarse[:, :LANES // 2], coarse[:, LANES // 2:])
    coarse_new[...] = coarse.astype(bf16)

    for n, off in ((8, -3), (10, 3), (12, 4)):
        arrived(n, off, 0)
        arrived(n + 1, off, 1)
        hand_over(off)

    if owners > 1:
        take(out_rows.at[pl.ds(1, owners - 1)], send_rows.at[0])
        take(out_tags.at[pl.ds(1, owners - 1)], send_tags.at[0])
    take(cnt_in.at[pl.ds(1, groups - 1)], send_cnt.at[0])
    take(num_out, send_num.at[0])
    for b in range(nz):
        take(sib_out.at[b], send_sib.at[b])
    for ref, sem in sent + ring:
        take(ref, sem)
    take(ring_new, send_gs.at[0])
    take(ring_new, keep.at[0])
    take(fine_new.at[other, :], recv_gs.at[0])


def per_device(owners, groups, embeddings, coarse_id, fine_count, fine):
    rows_dev, width = embeddings.shape
    f_own = fine.shape[0]
    nz = groups // 2
    assert nz == 8
    chunks = max(1, owners // 16)
    slots = owners * CAP
    bf16, f32 = jnp.bfloat16, jnp.float32
    vmem, dma = pltpu.VMEM, pltpu.SemaphoreType.DMA
    anywhere = pl.BlockSpec(memory_space=pl.ANY)
    tile = (f_own // 2, LANES)
    piece = (f_own // 4, LANES)
    return pl.pallas_call(
        functools.partial(kernel, owners, groups),
        out_shape=(
            jax.ShapeDtypeStruct((f_own, width), bf16),
            jax.ShapeDtypeStruct((KC_OWN, width // groups), bf16),
        ),
        in_specs=[anywhere] * 4,
        out_specs=(anywhere, pl.BlockSpec(memory_space=pltpu.VMEM)),
        scratch_shapes=[
            vmem((rows_dev, width), bf16),
            vmem((1, rows_dev), jnp.int32),
            vmem((1, KC_OWN), jnp.int32),
            vmem((f_own, width), bf16),
            vmem((owners, 2 * CAP, width // 2), bf16),
            vmem((owners, 2 * CAP, width // 2), bf16),
            vmem((owners, 1, LANES), f32),
            vmem((owners, 1, LANES), f32),
            vmem((nz, slots, LANES), bf16),
            vmem((f_own, slots), bf16),
            vmem((nz,) + tile, f32),
            vmem((nz,) + tile, bf16),
            vmem((nz,) + tile, bf16),
            vmem((2,) + piece, bf16),
            vmem((2,) + piece, bf16),
            vmem((2,) + tile, bf16),
            vmem((2,) + tile, bf16),
            vmem((2, 2) + piece, bf16),
            vmem((2, 2) + piece, bf16),
            vmem((2,) + tile, bf16),
            vmem((2,) + tile, bf16),
            vmem((1, f_own), f32),
            vmem((groups, 1, f_own), f32),
            vmem((KC_OWN, LANES), f32),
            vmem((KC_OWN, LANES), f32),
            vmem((f_own, LANES), f32),
            vmem((nz,) + tile, bf16),
            dma((4,)),
            dma((1,)), dma((chunks,)), dma((1,)), dma((chunks,)), dma((nz,)), dma((nz,)),
            dma((10,)), dma((10,)), dma((1,)), dma((1,)), dma((1,)), dma((1,)),
            dma((14,)), dma((14,)), dma((1,)), dma((1,)), dma((1,)),
        ],
        compiler_params=pltpu.CompilerParams(
            collective_id=0, has_side_effects=True, vmem_limit_bytes=56 * 1024 * 1024
        ),
    )(embeddings, coarse_id.reshape(1, rows_dev), fine_count, fine)


def solution(mesh):
    return jax.shard_map(
        functools.partial(per_device, mesh.shape["own"], mesh.shape["grp"]),
        mesh=mesh,
        in_specs=(P(("grp", "own"), None), P(("grp", "own")), P("own", None), P("own", None)),
        out_specs=(P("own", None), P("own", "grp")),
        check_vma=False,
    )
```

time: 93 us -> 79.7 us (0.86)
  Pallas kernels: 87.6 us -> 76.1 us
  local copies, waits for them, and re-layouts: 4.49 us -> 2.85 us
    pallas_call x1, Pallas kernels: 87.6 us -> 76.1 us  [per_device(): pl.pallas_call(functools.partial(kernel, owners, groups), out_shape=(jax....]
    unnamed x10 -> x4, local copies, waits for them, and re-layouts: 4.49 us -> 2.85 us
where the time goes in v2:
time: 79.7 us; the launch traced here: 79.6 us
  Pallas kernels  76.1 us (95%)
  local copies, waits for them, and re-layouts  2.85 us (4%)
    pallas_call x1, Pallas kernels, per_device(): pl.pallas_call(functools.partial(kernel, owners, groups), out_shape=(jax....  76.1 us
    unnamed x4, local copies, waits for them, and re-layouts  2.85 us

profile of v2, /device:TPU:1, one launch (start us, length us, event | category | flops | bytes accessed | tf_op | source)
XLA Modules:
  0.0 79.6 jit_solution(14743693391541564697)
XLA Ops:
  0.6 76.1 %shard_map.59 = (bf16[512,1024]{1,0:T(8,128)(2,1)}, bf16[8,64]{1,0:T(8,128)(2,1)}) custom-call(bf16[256,1024]{1,0:T(8,128)(2,1)} %emb_hbm.1, s32[1,256]{1,0:T(1,128)} %bitcast.1, s32[1,8]{1,0:T(1,128)} %count_hbm.1, bf16[512,1024]{1,0:T(8,128)(2,1)} %fine_hbm.1), custom_call_target="tpu_custom_call" | custom-call | tf_op jit(solution)/shard_map/pallas_call | solution.py:404
  76.7 0.0 copy-start
  76.7 2.3 %copy.8 = bf16[512,1024]{1,0:T(8,128)(2,1)} copy(bf16[512,1024]{1,0:T(8,128)(2,1)} %get-tuple-element.4) | data formatting | bytes 2097152
  79.0 0.0 copy-done
  79.0 0.6 copy.9
Async XLA Ops:
  76.7 2.3 %copy-start = (bf16[8,64]{1,0:T(8,128)(2,1)S(1)}, bf16[8,64]{1,0:T(8,128)(2,1)}, u32[]{:S(2)}) copy-start(bf16[8,64]{1,0:T(8,128)(2,1)} %get-tuple-element.5) | copy-start | bytes 3076

commit v3 on v2

--- a/solution.py
+++ b/solution.py
@@ -163,7 +163,8 @@
     in_tags[here] = out_tags[here]
 
     loads[1].wait()
-    for c in range(chunks):
+    @pl.loop(0, chunks)
+    def _(c):
         tall = 2 * CAP * chunk
         at = iota((tall, rows_dev), 0) + c * tall
         low = (at == target).astype(bf16)
@@ -198,11 +199,15 @@
     table[...] = jnp.broadcast_to(squares * 0.5, table.shape)
     member_of = (cluster_row == iota((KC_OWN, f_own), 0).astype(f32)).astype(f32)
 
-    for c in range(chunks):
-        gone = chunk - (1 if c == here // chunk else 0)
-        if gone > 0:
-            take(in_tags.at[pl.ds(c * chunk, gone)], recv_tags.at[c])
-            take(in_rows.at[pl.ds(c * chunk, gone)], recv_rows.at[c])
+    @pl.loop(0, chunks)
+    def _(c):
+        def come(count):
+            if count > 0:
+                take(in_tags.at[pl.ds(c * chunk, count)], recv_tags.at[c])
+                take(in_rows.at[pl.ds(c * chunk, count)], recv_rows.at[c])
+
+        pl.when(c == here // chunk)(functools.partial(come, chunk - 1))
+        pl.when(c != here // chunk)(functools.partial(come, chunk))
         these = pl.ds(c * chunk, chunk)
         tag = in_tags[these].reshape(chunk, LANES)[:, :slots]
         tag = jnp.where(iota((chunk, slots), 1) // CAP == iota((chunk, slots), 0), tag, 0.0)
@@ -210,7 +215,7 @@
         wide = in_rows[these].astype(f32).reshape(chunk, 2, CAP, half)
         low = wide[:, 0].reshape(slots, half).astype(bf16)
         high = wide[:, 1].reshape(slots, half).astype(bf16)
-        at = pl.ds(c * slots, slots)
+        at = pl.ds(pl.multiple_of(c * slots, slots), slots)
         for b in range(nz // 2):
             rows[b, at, :] = low[:, b * LANES:(b + 1) * LANES]
             rows[nz // 2 + b, at, :] = high[:, b * LANES:(b + 1) * LANES]
@@ -264,8 +269,10 @@
         take(ref, recv_sum.at[n])
         return ref[...].astype(f32)
 
-    for off in (4, 3, -3):
-        weigh(off)
+    @pl.loop(0, 3)
+    def _(n):
+        weigh(jnp.where(n == 0, 4, jnp.where(n == 1, 3, -3)))
+
     total = both(4).astype(bf16)
     for q, k in ((0, -2), (1, 2)):
         out4[q] = total[q * f_quarter:(q + 1) * f_quarter]
@@ -273,11 +280,11 @@
     for n, off, k in ((0, -3, -1), (1, 3, 1)):
         out3[n] = both(off).astype(bf16)
         give(2 + n, out3.at[n], in3.at[n], k)
-    for off in (2, -2):
-        weigh(off)
+    @pl.loop(0, 4)
+    def _(n):
+        weigh((2 - n // 2) * (1 - 2 * lax.rem(n, 2)))
+
     count_up()
-    for off in (1, -1):
-        weigh(off)
     for n, off in ((0, -1), (1, 1)):
         out1[n] = both(off).astype(bf16)
         give(4 + n, out1.at[n], in1.at[n], off)
@@ -370,11 +377,6 @@
     coarse = jnp.where(core == 0, coarse[:, :LANES // 2], coarse[:, LANES // 2:])
     coarse_new[...] = coarse.astype(bf16)
 
-    for n, off in ((8, -3), (10, 3), (12, 4)):
-        arrived(n, off, 0)
-        arrived(n + 1, off, 1)
-        hand_over(off)
-
     if owners > 1:
         take(out_rows.at[pl.ds(1, owners - 1)], send_rows.at[0])
         take(out_tags.at[pl.ds(1, owners - 1)], send_tags.at[0])
@@ -382,7 +384,15 @@
     take(num_out, send_num.at[0])
     for b in range(nz):
         take(sib_out.at[b], send_sib.at[b])
-    for ref, sem in sent + ring:
+    for ref, sem in sent:
+        take(ref, sem)
+
+    for n, off in ((8, -3), (10, 3), (12, 4)):
+        arrived(n, off, 0)
+        arrived(n + 1, off, 1)
+        hand_over(off)
+
+    for ref, sem in ring:
         take(ref, sem)
     take(ring_new, send_gs.at[0])
     take(ring_new, keep.at[0])

time: 79.7 us -> 79.2 us (level)
  no operation moved by 1% of the time
where the time goes in v3:
time: 79.2 us; the launch traced here: 79 us
  Pallas kernels  75.5 us (95%)
  local copies, waits for them, and re-layouts  2.85 us (4%)
    pallas_call x1, Pallas kernels, per_device(): pl.pallas_call(functools.partial(kernel, owners, groups), out_shape=(jax....  75.5 us
    unnamed x4, local copies, waits for them, and re-layouts  2.85 us

profile of v3, /device:TPU:1, one launch (start us, length us, event | category | flops | bytes accessed | tf_op | source)
XLA Modules:
  0.0 79.0 jit_solution(13687728909278636869)
XLA Ops:
  0.6 75.5 %shard_map.59 = (bf16[512,1024]{1,0:T(8,128)(2,1)}, bf16[8,64]{1,0:T(8,128)(2,1)}) custom-call(bf16[256,1024]{1,0:T(8,128)(2,1)} %emb_hbm.1, s32[1,256]{1,0:T(1,128)} %bitcast.1, s32[1,8]{1,0:T(1,128)} %count_hbm.1, bf16[512,1024]{1,0:T(8,128)(2,1)} %fine_hbm.1), custom_call_target="tpu_custom_call" | custom-call | tf_op jit(solution)/shard_map/pallas_call | solution.py:414
  76.1 0.0 copy-start
  76.2 2.3 %copy.8 = bf16[512,1024]{1,0:T(8,128)(2,1)} copy(bf16[512,1024]{1,0:T(8,128)(2,1)} %get-tuple-element.4) | data formatting | bytes 2097152
  78.4 0.0 copy-done
  78.4 0.6 copy.9
Async XLA Ops:
  76.1 2.3 %copy-start = (bf16[8,64]{1,0:T(8,128)(2,1)S(1)}, bf16[8,64]{1,0:T(8,128)(2,1)}, u32[]{:S(2)}) copy-start(bf16[8,64]{1,0:T(8,128)(2,1)} %get-tuple-element.5) | copy-start | bytes 3076

commit v4 on v3

--- a/solution.py
+++ b/solution.py
@@ -277,9 +277,12 @@
     for q, k in ((0, -2), (1, 2)):
         out4[q] = total[q * f_quarter:(q + 1) * f_quarter]
         give(q, out4.at[q], in4.at[q], k)
-    for n, off, k in ((0, -3, -1), (1, 3, 1)):
+    for n, off in ((0, -3), (1, 3)):
         out3[n] = both(off).astype(bf16)
-        give(2 + n, out3.at[n], in3.at[n], k)
+    for q in range(2):
+        piece = pl.ds(q * f_quarter, f_quarter)
+        for n, k in ((1, 1), (0, -1)):
+            give(2 + n + 8 * q, out3.at[n, piece, :], in3.at[n, piece, :], k)
     @pl.loop(0, 4)
     def _(n):
         weigh((2 - n // 2) * (1 - 2 * lax.rem(n, 2)))
@@ -291,11 +294,10 @@
     weigh(0)
     for off in (-2, 2, 0):
         take(sib_in.at[along(off)], recv_sib.at[along(off)])
-    for n, off in ((0, -2), (1, 2)):
-        take(in3.at[n], recv_sum.at[2 + n])
     for q in range(2):
+        piece = pl.ds(q * f_quarter, f_quarter)
         for n, off in ((1, 2), (0, -2)) if q == 0 else ((0, -2), (1, 2)):
-            total = chip(off, q) + in3[n, pl.ds(q * f_quarter, f_quarter), :].astype(f32)
+            total = chip(off, q) + got(2 + n + 8 * q, in3.at[n, piece, :])
             if n == q:
                 total += got(q, in4.at[q])
             out2[n, q] = total.astype(bf16)
@@ -449,7 +451,7 @@
             vmem((nz,) + tile, bf16),
             dma((4,)),
             dma((1,)), dma((chunks,)), dma((1,)), dma((chunks,)), dma((nz,)), dma((nz,)),
-            dma((10,)), dma((10,)), dma((1,)), dma((1,)), dma((1,)), dma((1,)),
+            dma((12,)), dma((12,)), dma((1,)), dma((1,)), dma((1,)), dma((1,)),
             dma((14,)), dma((14,)), dma((1,)), dma((1,)), dma((1,)),
         ],
         compiler_params=pltpu.CompilerParams(

time: 79.2 us -> 80.1 us (1.011)
  Pallas kernels: 75.5 us -> 76.5 us
    pallas_call x1, Pallas kernels: 75.5 us -> 76.5 us  [per_device(): pl.pallas_call(functools.partial(kernel, owners, groups), out_shape=(jax....]
where the time goes in v4:
time: 80.1 us; the launch traced here: 80 us
  Pallas kernels  76.5 us (96%)
  local copies, waits for them, and re-layouts  2.85 us (4%)
    pallas_call x1, Pallas kernels, per_device(): pl.pallas_call(functools.partial(kernel, owners, groups), out_shape=(jax....  76.5 us
    unnamed x4, local copies, waits for them, and re-layouts  2.85 us

profile of v4, /device:TPU:1, one launch (start us, length us, event | category | flops | bytes accessed | tf_op | source)
XLA Modules:
  0.0 80.0 jit_solution(17133811394781165003)
XLA Ops:
  0.6 76.5 %shard_map.59 = (bf16[512,1024]{1,0:T(8,128)(2,1)}, bf16[8,64]{1,0:T(8,128)(2,1)}) custom-call(bf16[256,1024]{1,0:T(8,128)(2,1)} %emb_hbm.1, s32[1,256]{1,0:T(1,128)} %bitcast.1, s32[1,8]{1,0:T(1,128)} %count_hbm.1, bf16[512,1024]{1,0:T(8,128)(2,1)} %fine_hbm.1), custom_call_target="tpu_custom_call" | custom-call | tf_op jit(solution)/shard_map/pallas_call | solution.py:416
  77.1 0.0 copy-start
  77.1 2.3 %copy.8 = bf16[512,1024]{1,0:T(8,128)(2,1)} copy(bf16[512,1024]{1,0:T(8,128)(2,1)} %get-tuple-element.4) | data formatting | bytes 2097152
  79.4 0.0 copy-done
  79.4 0.6 copy.9
Async XLA Ops:
  77.1 2.3 %copy-start = (bf16[8,64]{1,0:T(8,128)(2,1)S(1)}, bf16[8,64]{1,0:T(8,128)(2,1)}, u32[]{:S(2)}) copy-start(bf16[8,64]{1,0:T(8,128)(2,1)} %get-tuple-element.5) | copy-start | bytes 3076
